TPU v7x, 256 devices: a whole 4x4x8 slice. The times are simulated.
256 devices in a mesh: gx: 32 (over x_lo, z, core), gy: 8 (over y, x_hi).
Axes of the slice: x: 4 (x_hi: 2, x_lo: 2; x = x_hi * 2 + x_lo), y: 4, z: 8, core: 2. Of those that a mesh axis runs over, the one named last changes fastest.
Arguments:
- body_force: float32 [3, 512, 128, 256], P(None, 'gx', 'gy'), may hold values from -6 to 6
- phase: int32 [512, 128, 256], P('gx', 'gy'), may hold values from 0 to 7
- viscosity_table: float32 [8], replicated, may hold values from 0.001 to 1000
- wall_kinds: int32 [3, 6], replicated, may hold values from 0 to 1
Outputs:
- weighted_velocity: float32 [3, 512, 128, 256], P(None, 'gx', 'gy')
- residual: float32 [3, 512, 128, 256], P(None, 'gx', 'gy')
Inputs may be any that keep to these rules, and one draw needn't show every extreme that they name: phase values are valid indices 0 to 7 into viscosity_table.
All inputs are finite; a program needn't handle non-finite values.
Results may differ from a plain program's by a relative error of at most 0.0003.
Values sent between devices are 32-bit elements; how exact they have to be, the bound alone decides.
A program may use at most 320 MiB of HBM per device.

v0:
```python
import jax
import jax.numpy as jnp
from jax import lax
from jax.sharding import PartitionSpec as P

LEVELS = 4
SWEEPS = 2
CSWEEPS = 24


fine_low = 0.2
fine_high = 2.0
coarse_low = 0.05
coarse_high = 2.0


def with_halo(cells, sides, width):
    for axis, dim in sides:
        count = lax.axis_size(axis)
        ends = count - 1
        head = lax.slice_in_dim(cells, 0, width, axis=dim)
        tail = lax.slice_in_dim(cells, cells.shape[dim] - width, cells.shape[dim], axis=dim)
        cells = jnp.concatenate(
            [
                lax.ppermute(tail, axis, [(i, (i + 1) % count) for i in range(ends)]),
                cells,
                lax.ppermute(head, axis, [((i + 1) % count, i) for i in range(ends)]),
            ],
            axis=dim,
        )
    return cells


def wall_terms(viscosity, x_places, y_places, z_count, x_total, y_total, wall_kinds, scale):
    kinds = wall_kinds.astype(jnp.float32)
    z_places = jnp.arange(z_count, dtype=jnp.int32)
    x_low = (x_places == 0).astype(jnp.float32)[:, None, None]
    x_high = (x_places == x_total - 1).astype(jnp.float32)[:, None, None]
    y_low = (y_places == 0).astype(jnp.float32)[None, :, None]
    y_high = (y_places == y_total - 1).astype(jnp.float32)[None, :, None]
    z_low = (z_places == 0).astype(jnp.float32)[None, None, :]
    z_high = (z_places == z_count - 1).astype(jnp.float32)[None, None, :]
    total = kinds[:, 0, None, None, None] * x_low[None]
    total = total + kinds[:, 1, None, None, None] * x_high[None]
    total = total + kinds[:, 2, None, None, None] * y_low[None]
    total = total + kinds[:, 3, None, None, None] * y_high[None]
    total = total + kinds[:, 4, None, None, None] * z_low[None]
    total = total + kinds[:, 5, None, None, None] * z_high[None]
    return 2.0 * scale * viscosity[None] * total


def halve(values):
    lead = values.shape[:-3]
    x_count, y_count, z_count = values.shape[-3:]
    split = values.reshape(lead + (x_count // 2, 2, y_count // 2, 2, z_count // 2, 2))
    return jnp.mean(split, axis=(-5, -3, -1))


def widen(values):
    comps, x_count, y_count, z_count = values.shape
    spread = jnp.broadcast_to(
        values.reshape(comps, x_count, 1, y_count, 1, z_count, 1),
        (comps, x_count, 2, y_count, 2, z_count, 2),
    )
    return spread.reshape(comps, 2 * x_count, 2 * y_count, 2 * z_count)


def build_block(rimmed, width, x_start, y_start, x_total, y_total, wall_kinds, scale):
    x_count, y_count, z_count = rimmed.shape
    x_places = x_start + jnp.arange(x_count, dtype=jnp.int32)
    y_places = y_start + jnp.arange(y_count, dtype=jnp.int32)
    inside = ((x_places >= 0) & (x_places < x_total))[:, None] & (
        (y_places >= 0) & (y_places < y_total)
    )[None, :]
    inner = jnp.where(inside[:, :, None], rimmed, 0.0)
    pair_x = (inside[:-1] & inside[1:])[:, :, None]
    pair_y = (inside[:, :-1] & inside[:, 1:])[:, :, None]
    face_x = jnp.where(pair_x, 0.5 * (inner[:-1] + inner[1:]) * scale, 0.0)
    face_y = jnp.where(pair_y, 0.5 * (inner[:, :-1] + inner[:, 1:]) * scale, 0.0)
    face_z = 0.5 * (inner[:, :, :-1] + inner[:, :, 1:]) * scale
    zero_z = jnp.zeros((x_count, y_count, 1), jnp.float32)
    sum_x = (face_x[:-1] + face_x[1:])[:, 1:-1]
    sum_y = (face_y[:, :-1] + face_y[:, 1:])[1:-1]
    sum_z = (jnp.concatenate([zero_z, face_z], 2) + jnp.concatenate([face_z, zero_z], 2))[
        1:-1, 1:-1
    ]
    walls = wall_terms(
        inner[1:-1, 1:-1],
        x_places[1:-1],
        y_places[1:-1],
        z_count,
        x_total,
        y_total,
        wall_kinds,
        scale,
    )
    diagonal = jnp.where(inside[1:-1, 1:-1, None][None], (sum_x + sum_y + sum_z)[None] + walls, 1.0)
    return (face_x, face_y, face_z, diagonal, width)


def diagonal_at(level):
    diagonal = level[3]
    return diagonal


def apply_block(field, level, margin):
    face_x, face_y, face_z, diagonal, width = level
    x_out = field.shape[1] - 2
    y_out = field.shape[2] - 2
    start = width - margin + 1
    center = field[:, 1 : 1 + x_out, 1 : 1 + y_out]
    near = (
        face_x[start - 1 : start - 1 + x_out, start : start + y_out]
        * field[:, 0:x_out, 1 : 1 + y_out]
        + face_x[start : start + x_out, start : start + y_out]
        * field[:, 2 : 2 + x_out, 1 : 1 + y_out]
    )
    near = (
        near
        + face_y[start : start + x_out, start - 1 : start - 1 + y_out]
        * field[:, 1 : 1 + x_out, 0:y_out]
        + face_y[start : start + x_out, start : start + y_out]
        * field[:, 1 : 1 + x_out, 2 : 2 + y_out]
    )
    vertical = face_z[start : start + x_out, start : start + y_out]
    zero_z = jnp.zeros((field.shape[0], x_out, y_out, 1), jnp.float32)
    lower = jnp.concatenate([zero_z, vertical * center[..., :-1]], 3)
    upper = jnp.concatenate([vertical * center[..., 1:], zero_z], 3)
    near = near + lower + upper
    return diagonal * center - near


def smooth_block(resid, level, low, high, sweeps, grow_each):
    middle = (high + low) / 2.0
    radius = (high - low) / 2.0
    relative = middle / radius
    ratio_now = 1.0 / relative
    step = resid / (middle * diagonal_at(level))
    field = jnp.zeros_like(step)
    for sweep_index in range(sweeps):
        field = field + step
        image = apply_block(grow_each(step), level, 1)
        resid = resid - image
        if sweep_index < sweeps - 1:
            ratio_next = 1.0 / (2.0 * relative - ratio_now)
            step = ratio_next * ratio_now * step + 2.0 * ratio_next / radius * (
                resid / diagonal_at(level)
            )
            ratio_now = ratio_next
    return (field, resid)


def per_device(body_force, phase, viscosity_table, wall_kinds):
    viscosity = jnp.zeros(phase.shape, jnp.float32)
    for phase_index in range(viscosity_table.shape[0]):
        viscosity = viscosity + jnp.where(phase == phase_index, viscosity_table[phase_index], 0.0)
    x_devices = lax.axis_size("gx")
    y_devices = lax.axis_size("gy")
    x_rank = lax.axis_index("gx")
    y_rank = lax.axis_index("gy")
    width = 1

    def grow_each(values):
        return with_halo(values, (("gx", 1), ("gy", 2)), 1)

    levels = []
    for level_index in range(LEVELS - 1):
        x_cells = viscosity.shape[0]
        y_cells = viscosity.shape[1]
        rimmed = with_halo(viscosity, (("gx", 0), ("gy", 1)), width)
        levels.append(
            build_block(
                rimmed,
                width,
                x_rank * x_cells - width,
                y_rank * y_cells - width,
                x_cells * x_devices,
                y_cells * y_devices,
                wall_kinds,
                0.25**level_index,
            )
        )
        viscosity = halve(viscosity)
    resid = body_force
    fields = []
    resids = []
    for level_index in range(LEVELS - 1):
        field, resid = smooth_block(
            resid, levels[level_index], fine_low, fine_high, SWEEPS, grow_each
        )
        fields.append(field)
        resids.append(resid)
        resid = halve(resid)
    coarse_scale = 0.25 ** (LEVELS - 1)
    x_cells = resid.shape[1]
    y_cells = resid.shape[2]
    column_resid, column_visc = (
        lax.all_gather(resid, "gy", axis=2, tiled=True),
        lax.all_gather(viscosity, "gy", axis=1, tiled=True),
    )

    def grow_coarse(values):
        wider = with_halo(values, (("gx", 1),), 1)
        return jnp.pad(wider, ((0, 0), (0, 0), (1, 1), (0, 0)))

    coarse_rimmed = grow_coarse(column_visc[None])[0]
    coarse_level = build_block(
        coarse_rimmed,
        1,
        x_rank * x_cells - 1,
        -1,
        x_cells * x_devices,
        y_cells * y_devices,
        wall_kinds,
        coarse_scale,
    )
    coarse_field, unused = smooth_block(
        column_resid, coarse_level, coarse_low, coarse_high, CSWEEPS, grow_coarse
    )
    correction = lax.dynamic_slice_in_dim(coarse_field, y_rank * y_cells, y_cells, 2)
    for level_index in reversed(range(LEVELS - 1)):
        lifted = widen(correction)
        rimmed_lift = with_halo(lifted, (("gx", 1), ("gy", 2)), 1)
        resid = resids[level_index] - apply_block(rimmed_lift, levels[level_index], 1)
        extra, resid = smooth_block(
            resid, levels[level_index], fine_low, fine_high, SWEEPS, grow_each
        )
        correction = fields[level_index] + lifted + extra
    return (diagonal_at(levels[0]) * correction, resid)


def solution(mesh):
    placed = (P(None, "gx", "gy", None), P("gx", "gy", None), P(), P())
    return jax.shard_map(
        per_device,
        mesh=mesh,
        in_specs=placed,
        out_specs=(P(None, "gx", "gy", None), P(None, "gx", "gy", None)),
        check_vma=False,
    )
```

profile of v0, /device:TPU:2, one launch (start us, length us, event | category | flops | bytes accessed | tf_op | source)
XLA Modules:
  0.0 833.0 jit_solution(4039657371741923894)
XLA Ops:
  2.3 6.3 select_add_fusion
  11.1 7.2 collective-permute-start.1
  18.3 18.1 %reshape.1100 = f32[8,2,8,2,128,2]{5,4,3,2,1,0:T(8,128)} reshape(f32[16,16,256]{2,1,0:T(8,128)S(1)} %select_add_fusion) | data formatting | bytes 524288 | tf_op jit(solution)/shard_map/reshape | solution.py:55
  36.4 7.0 reduce_sum.55
  50.2 5.8 collective-permute-start.25
  58.5 31.0 %all_gather.7 = f32[2,16,32]{2,0,1:T(2,128)S(1)} all-gather(f32[2,2,32]{2,0,1:T(2,128)S(1)} %copy.10), channel_id=1, replica_groups=mesh['gx'=32,'gy'=8] {'gy'}, dimensions={1}, use_global_device_ids=true | all-gather | bytes 4608 | tf_op jit(solution)/shard_map/all_gather | solution.py:199
  97.2 5.8 collective-permute-start.37
  121.9 6.0 collective-permute-done.15
  129.9 6.3 collective-permute-start.2
  147.4 5.8 collective-permute-start.5
  159.6 5.8 collective-permute-done.7
  169.0 5.8 collective-permute-start.9
  191.7 51.7 %reshape.1099 = f32[3,8,2,8,2,128,2]{6,5,4,3,2,1,0:T(8,128)} reshape(f32[3,16,16,256]{3,2,1,0:T(8,128)S(1)} %fusion.38) | data formatting | bytes 1572864 | tf_op jit(solution)/shard_map/reshape | solution.py:55
  243.4 18.4 %reduce_sum.54 = f32[3,8,8,128]{3,2,1,0:T(8,128)} reduce(f32[3,8,2,8,2,128,2]{6,5,4,3,2,1,0:T(8,128)} %reshape.1099, f32[]{:T(128)} %constant.90.clone.1), dimensions={2,4,6}, to_apply=%region_0.1 | reduce | flops 172032 | bytes 884740 | tf_op jit(solution)/shard_map/reduce_sum | solution.py:56
  264.9 5.8 collective-permute-start.17
  285.6 5.8 collective-permute-start.21
  306.2 7.7 reshape.1101
  319.9 5.8 collective-permute-start.29
  340.0 5.8 collective-permute-start.33
  361.2 34.4 %all_gather.6 = f32[3,2,16,32]{3,1,0,2:T(2,128)S(1)} all-gather(f32[3,2,2,32]{3,1,0,2:T(2,128)S(1)} %copy.9), channel_id=1, replica_groups=mesh['gx'=32,'gy'=8] {'gy'}, dimensions={2}, use_global_device_ids=true | all-gather | bytes 13824 | tf_op jit(solution)/shard_map/all_gather | solution.py:198
  397.8 5.8 collective-permute-start.39
  407.4 5.8 collective-permute-start.41
  417.0 5.8 collective-permute-start.43
  436.2 5.8 collective-permute-start.47
  445.8 5.8 collective-permute-start.49
  455.4 5.9 collective-permute-start.51
  710.0 16.5 %broadcast_in_dim.280 = f32[3,8,2,8,2,128,2]{6,5,4,3,2,1,0:T(8,128)} broadcast(f32[3,8,8,128]{3,2,1,0:T(8,128)S(1)} %add_add_fusion), dimensions={0,1,3,5} | broadcast | bytes 884736 | tf_op jit(solution)/shard_map/broadcast_in_dim | solution.py:61
  726.5 35.6 %reshape.1105 = f32[3,16,16,256]{3,2,1,0:T(8,128)S(1)} reshape(f32[3,8,2,8,2,128,2]{6,5,4,3,2,1,0:T(8,128)} %broadcast_in_dim.280) | data formatting | bytes 1572864 | tf_op jit(solution)/shard_map/reshape | solution.py:65
  777.7 5.8 collective-permute-done.103
  795.1 6.3 collective-permute-start.106
  803.2 5.8 collective-permute-done.107
  824.8 5.8 collective-permute-done.111
  (585 shorter events, 472.8 us)
Async XLA Ops:
  9.2 120.0 %collective-permute-start = (f32[1,16,256]{2,1,0:T(8,128)}, f32[1,16,256]{2,1,0:T(8,128)}, u32[]{:S(2)}, u32[]{:S(2)}) collective-permute-start(f32[1,16,256]{2,1,0:T(8,128)} %get-tuple-element.110), channel_id=1, source_target_pairs={{0,8},{8,16},{16,24},{24,32},{32,40},{40,48},{48,56},{56,64},{64,7... | collective-permute-start | bytes 49160 | tf_op jit(solution)/shard_map/ppermute | solution.py:25
  11.1 118.0 %collective-permute-start.1 = (f32[1,16,256]{2,1,0:T(8,128)}, f32[1,16,256]{2,1,0:T(8,128)}, u32[]{:S(2)}, u32[]{:S(2)}) collective-permute-start(f32[1,16,256]{2,1,0:T(8,128)} %get-tuple-element.111), channel_id=1, source_target_pairs={{8,0},{16,8},{24,16},{32,24},{40,32},{48,40},{56,48},{64,56},{72,6... | collective-permute-start | bytes 49160 | tf_op jit(solution)/shard_map/ppermute | solution.py:27
  44.0 70.7 %collective-permute-start.12 = (f32[1,8,128]{2,1,0:T(8,128)}, f32[1,8,128]{2,1,0:T(8,128)}, u32[]{:S(2)}, u32[]{:S(2)}) collective-permute-start(f32[1,8,128]{2,1,0:T(8,128)} %get-tuple-element.262), channel_id=1, source_target_pairs={{0,8},{8,16},{16,24},{24,32},{32,40},{40,48},{48,56},{56,64},{64,7... | collective-permute-start | bytes 12296 | tf_op jit(solution)/shard_map/ppermute | solution.py:25
  48.3 47.0 %collective-permute-start.24 = (f32[1,4,64]{2,1,0:T(4,128)S(1)}, f32[1,4,64]{2,1,0:T(4,128)S(1)}, u32[]{:S(2)}, u32[]{:S(2)}) collective-permute-start(f32[1,4,64]{2,1,0:T(4,128)S(1)} %get-tuple-element.284), channel_id=1, source_target_pairs={{0,8},{8,16},{16,24},{24,32},{32,40},{40,48},{48,56},{56,64},{64,7... | collective-permute-start | bytes 3080 | tf_op jit(solution)/shard_map/ppermute | solution.py:25
  50.2 47.0 %collective-permute-start.25 = (f32[1,4,64]{2,1,0:T(4,128)S(1)}, f32[1,4,64]{2,1,0:T(4,128)S(1)}, u32[]{:S(2)}, u32[]{:S(2)}) collective-permute-start(f32[1,4,64]{2,1,0:T(4,128)S(1)} %get-tuple-element.285), channel_id=1, source_target_pairs={{8,0},{16,8},{24,16},{32,24},{40,32},{48,40},{56,48},{64,56},{72,6... | collective-permute-start | bytes 3080 | tf_op jit(solution)/shard_map/ppermute | solution.py:27
  97.2 10.1 %collective-permute-start.37 = (f32[1,1,16,32]{3,1,2,0:T(1,128)S(1)}, f32[1,1,16,32]{3,1,2,0:T(1,128)S(1)}, u32[]{:S(2)}, u32[]{:S(2)}) collective-permute-start(f32[1,1,16,32]{3,1,2,0:T(1,128)S(1)} %get-tuple-element.281), channel_id=1, source_target_pairs={{8,0},{16,8},{24,16},{32,24},{40,32},{48,40},{56,48},{64,56},{72,6... | collective-permute-start | bytes 6152 | tf_op jit(solution)/shard_map/ppermute | solution.py:27
  120.0 7.9 collective-permute-start.15
  129.9 8.3 collective-permute-start.2
  145.4 8.0 collective-permute-start.4
  263.0 9.5 %collective-permute-start.16 = (f32[3,1,8,128]{3,2,1,0:T(8,128)S(1)}, f32[3,1,8,128]{3,2,1,0:T(8,128)S(1)}, u32[]{:S(2)}, u32[]{:S(2)}) collective-permute-start(f32[3,1,8,128]{3,2,1,0:T(8,128)S(1)} %get-tuple-element.134), channel_id=1, source_target_pairs={{0,8},{8,16},{16,24},{24,32},{32,40},{40,48},{48,56},{56,64},{64,7... | collective-permute-start | bytes 36872 | tf_op jit(solution)/shard_map/ppermute | solution.py:25
  318.0 9.2 %collective-permute-start.28 = (f32[3,1,4,64]{3,2,1,0:T(4,128)S(1)}, f32[3,1,4,64]{3,2,1,0:T(4,128)S(1)}, u32[]{:S(2)}, u32[]{:S(2)}) collective-permute-start(f32[3,1,4,64]{3,2,1,0:T(4,128)S(1)} %get-tuple-element.272), channel_id=1, source_target_pairs={{0,8},{8,16},{16,24},{24,32},{32,40},{40,48},{48,56},{56,64},{64,7... | collective-permute-start | bytes 9224 | tf_op jit(solution)/shard_map/ppermute | solution.py:25
  338.0 9.4 %collective-permute-start.32 = (f32[3,1,4,64]{3,2,1,0:T(4,128)S(1)}, f32[3,1,4,64]{3,2,1,0:T(4,128)S(1)}, u32[]{:S(2)}, u32[]{:S(2)}) collective-permute-start(f32[3,1,4,64]{3,2,1,0:T(4,128)S(1)} %get-tuple-element.268), channel_id=1, source_target_pairs={{0,8},{8,16},{16,24},{24,32},{32,40},{40,48},{48,56},{56,64},{64,7... | collective-permute-start | bytes 9224 | tf_op jit(solution)/shard_map/ppermute | solution.py:25
  395.8 7.8 collective-permute-start.38
  405.5 7.8 collective-permute-start.40
  415.1 7.8 collective-permute-start.42
  424.7 7.8 collective-permute-start.44
  434.3 7.8 collective-permute-start.46
  443.9 7.8 collective-permute-start.48
  453.5 8.0 collective-permute-start.50
  463.1 7.8 collective-permute-start.52
  472.7 7.8 collective-permute-start.54
  482.3 7.8 collective-permute-start.56
  491.9 7.8 collective-permute-start.58
  511.1 7.8 collective-permute-start.62
  520.6 7.8 collective-permute-start.64
  530.2 7.8 collective-permute-start.66
  549.4 7.8 collective-permute-start.70
  559.2 7.8 collective-permute-start.72
  644.7 8.0 collective-permute-start.90
  762.1 7.8 collective-permute-start.100
  795.1 8.1 collective-permute-start.106
  810.7 9.3 %collective-permute-start.108 = (f32[3,1,16,256]{3,2,1,0:T(8,128)S(1)}, f32[3,1,16,256]{3,2,1,0:T(8,128)S(1)}, u32[]{:S(2)}, u32[]{:S(2)}) collective-permute-start(f32[3,1,16,256]{3,2,1,0:T(8,128)S(1)} %get-tuple-element.90), channel_id=1, source_target_pairs={{0,8},{8,16},{16,24},{24,32},{32,40},{40,48},{48,56},{56,64},{64,7... | collective-permute-start | bytes 147464 | tf_op jit(solution)/shard_map/ppermute | solution.py:25
  (126 other events, 4050.2 us)
where the time goes:
time: 846 us; the launch traced here: 833 us
  starting transfers between devices  392 us (46%)
  local copies, waits for them, and re-layouts  156 us (18%)
  waiting for transfers between devices  130 us (15%)
  other arithmetic  85.8 us (10%)
  blocking collectives  65.4 us (8%)
    ppermute x56, starting transfers between devices, with_halo(): lax.ppermute(head, axis, [((i + 1) % count, i) for i in range(ends)])  250 us
    ppermute x56, starting transfers between devices, with_halo(): lax.ppermute(tail, axis, [(i, (i + 1) % count) for i in range(ends)])  142 us
    ppermute x56, waiting for transfers between devices, with_halo(): lax.ppermute(head, axis, [((i + 1) % count, i) for i in range(ends)])  128 us
    reshape x4, local copies, waits for them, and re-layouts, halve(): values.reshape(lead + (x_count // 2, 2, y_count // 2, 2, z_count // 2, 2))  79.1 us
    reshape x3, local copies, waits for them, and re-layouts, widen(): return spread.reshape(comps, 2 * x_count, 2 * y_count, 2 * z_count)  41.6 us
    all_gather x1, blocking collectives, per_device(): lax.all_gather(resid, 'gy', axis=2, tiled=True)  34.4 us
    all_gather x1, blocking collectives, per_device(): lax.all_gather(viscosity, 'gy', axis=1, tiled=True)  31 us
    reduce_sum x6, other arithmetic, halve(): return jnp.mean(split, axis=(-5, -3, -1))  30.4 us
  transfers between devices with their start and end apart: 112, of which 53 were waited for; matrix products, arithmetic and copies ran while one was open for 7% of the time, Pallas kernels for 0%

commit v1 on v0

v1 whole, which is shorter than its diff:
```python
import jax
import jax.numpy as jnp
from jax import lax
from jax.experimental import pallas as pl
from jax.experimental.pallas import tpu as pltpu
from jax.sharding import PartitionSpec as P


F32 = jnp.float32
MESH = pl.DeviceIdType.MESH
LEVELS = 4
CSWEEPS = 24
NX = 32
NY = 8
LOW, HIGH = 0.2, 2.0
CLOW, CHIGH = 0.05, 2.0

MID = (HIGH + LOW) / 2.0
RAD = (HIGH - LOW) / 2.0
SIG = MID / RAD
RHO0 = 1.0 / SIG
RHO1 = 1.0 / (2.0 * SIG - RHO0)
STEP_A = RHO1 * RHO0
STEP_B = 2.0 * RHO1 / RAD

CMID = (CHIGH + CLOW) / 2.0
CRAD = (CHIGH - CLOW) / 2.0
CSIG = CMID / CRAD

SIDES = [(dx, dy) for dx in (-1, 0, 1) for dy in (-1, 0, 1) if dx or dy]
PAD = 4
BLOCK = 4
CHUNK = 8


def lanes():
    return lax.broadcasted_iota(jnp.int32, (8, 128), 1)


def subs():
    return lax.broadcasted_iota(jnp.int32, (8, 128), 0)


def tiled(index, values):
    return jnp.broadcast_to(index, values.shape)


def roll_lane(values, shift):
    return pltpu.roll(values, shift % 128, values.ndim - 1)


def roll_sub(values, shift):
    return pltpu.roll(values, shift % 8, values.ndim - 2)


def pick_lane(values, index):
    return jnp.take_along_axis(values, tiled(index, values), axis=values.ndim - 1, mode="promise_in_bounds")


def choose(mask, one, other):
    return jnp.where(tiled(mask, one), one, other)


def above(values, reach):
    moved = roll_lane(values, -reach)
    return choose(lanes() >= 128 - reach, roll_sub(moved, -1), moved)


def below(values, reach):
    moved = roll_lane(values, reach)
    return choose(lanes() < reach, roll_sub(moved, 1), moved)


def pair_sum(values, reach):
    return values + choose((lanes() & reach) == 0, roll_lane(values, -reach), roll_lane(values, reach))


def spread_sub(values, group):
    kept = jnp.where(tiled(subs() // 2 == group, values), values, 0.0)
    kept = kept + roll_sub(kept, 2)
    return kept + roll_sub(kept, 4)


def by_group(parts):
    group = subs() // 2
    out = parts[3]
    for k in (2, 1, 0):
        out = choose(group == k, parts[k], out)
    return out


def quad(lo, hi):
    return [(j, min(CHUNK, hi - j)) for j in range(lo, hi, CHUNK)]


def loop(lo, hi, body):
    def step(i, carry):
        body(i)
        return carry

    lax.fori_loop(lo, hi, step, 0)


class Level:
    def __init__(self, index, block, halo, refs):
        self.block, self.halo = block, halo
        self.frame = block + 2 * halo
        self.reach = 2**index
        self.scale = 0.25**index
        self.V, self.KX, self.KY, self.KZ, self.D, self.I, self.R, self.SA, self.SB, self.Q, self.X, self.PR = refs

    def near(self, ref, i, j, m):
        wide = ref[i, pl.ds(j - 1, m + 2)]
        mid = wide[1:-1]
        ky = self.KY[i, pl.ds(j, m + 1)]
        kz = self.KZ[i, pl.ds(j, m)]
        out = self.KX[i, pl.ds(j, m)] * ref[i - 1, pl.ds(j, m)]
        out = out + self.KX[i + 1, pl.ds(j, m)] * ref[i + 1, pl.ds(j, m)]
        out = out + (ky[:-1] * wide[:-2] + ky[1:] * wide[2:])
        out = out + (kz * above(mid, self.reach) + below(kz * mid, self.reach))
        return mid, out

    def build(self, gx, gy, kinds, lo, hi):
        h, b = self.halo, self.block
        half = 0.5 * self.scale
        group, side = subs() // 2, subs() % 2

        def per_kind(wall):
            tile = jnp.zeros((8, 128), F32)
            for c in range(3):
                tile = jnp.where(group == c, kinds[c, wall].astype(F32), tile)
            return tile

        walls = [per_kind(wall) for wall in range(6)]
        z_low = (side == 0) & (lanes() < self.reach)
        z_high = (side == 1) & (lanes() >= 128 - self.reach)
        z_wall = jnp.where(z_low, walls[4], 0.0) + jnp.where(z_high, walls[5], 0.0)
        one, zero = jnp.float32(1.0), jnp.float32(0.0)
        at_x = (jnp.where(gx == 0, one, zero), jnp.where(gx == NX - 1, one, zero))
        at_y = (jnp.where(gy == 0, one, zero), jnp.where(gy == NY - 1, one, zero))

        def faces(i):
            place = gx * b + i - h
            open_x = jnp.where((place == 0) | (place == NX * b), zero, one)
            for j, m in quad(lo, hi):
                here = self.V[i, pl.ds(j, m)]
                self.KX[i, pl.ds(j, m)] = (half * open_x) * (self.V[i - 1, pl.ds(j, m)] + here)

        loop(lo, hi + 1, faces)

        def rest(i):
            x_wall = z_wall + jnp.where(i == h, at_x[0], zero) * walls[0]
            x_wall = x_wall + jnp.where(i == h + b - 1, at_x[1], zero) * walls[1]
            for j, m in quad(lo, hi + 1):
                self.KY[i, pl.ds(j, m)] = half * (self.V[i, pl.ds(j - 1, m)] + self.V[i, pl.ds(j, m)])
            self.KY[i, h] = self.KY[i, h] * (one - at_y[0])
            self.KY[i, h + b] = self.KY[i, h + b] * (one - at_y[1])
            for j, m in quad(lo, hi):
                here = self.V[i, pl.ds(j, m)]
                ky = self.KY[i, pl.ds(j, m + 1)]
                kz = half * (here + above(here, self.reach))
                kz = jnp.where(tiled(z_high, kz), 0.0, kz)
                self.KZ[i, pl.ds(j, m)] = kz
                total = self.KX[i, pl.ds(j, m)] + self.KX[i + 1, pl.ds(j, m)] + (ky[:-1] + ky[1:])
                total = total + (kz + below(kz, self.reach))
                self.D[i, pl.ds(j, m)] = total + (2.0 * self.scale) * here * tiled(x_wall, here)
            for j, wall, at in ((h, walls[2], at_y[0]), (h + b - 1, walls[3], at_y[1])):
                self.D[i, j] = self.D[i, j] + (2.0 * self.scale * at) * self.V[i, j] * wall
            for j, m in quad(lo, hi):
                self.I[i, pl.ds(j, m)] = 1.0 / self.D[i, pl.ds(j, m)]

        loop(lo, hi, rest)

    def first_step(self, src, lo, hi):
        def body(i):
            for j, m in quad(lo, hi):
                self.SA[i, pl.ds(j, m)] = src[i, pl.ds(j, m)] * self.I[i, pl.ds(j, m)] * (1.0 / MID)

        loop(lo, hi, body)

    def second_step(self, src, dst, lo, hi):
        def body(i):
            for j, m in quad(lo, hi):
                step, near = self.near(self.SA, i, j, m)
                r = src[i, pl.ds(j, m)] * (1.0 - 1.0 / MID) + near
                dst[i, pl.ds(j, m)] = r
                self.SB[i, pl.ds(j, m)] = STEP_A * step + STEP_B * (r * self.I[i, pl.ds(j, m)])

        loop(lo, hi, body)

    def descend(self):
        h, b = self.halo, self.block
        self.first_step(self.R, h - 2, h + b + 2)
        self.second_step(self.R, self.Q, h - 1, h + b + 1)

        def body(i):
            for j, m in quad(h, h + b):
                step, near = self.near(self.SB, i, j, m)
                self.Q[i, pl.ds(j, m)] = self.Q[i, pl.ds(j, m)] - self.D[i, pl.ds(j, m)] * step + near
                self.X[i, pl.ds(j, m)] = self.SA[i, pl.ds(j, m)] + step

        loop(h, h + b, body)

    def lift(self, ref, shift, first, count):
        def body(i):
            row = ref[(i + shift[0]) // 2 + shift[1], pl.ds(first, count)]
            row = jnp.broadcast_to(row[:, None], (count, 2, 8, 128)).reshape(2 * count, 8, 128)
            skip = (2 * count - self.frame) // 2
            self.PR[i] = row[skip : skip + self.frame]

        loop(0, self.frame, body)

    def correct(self, lo, hi):
        def body(i):
            for j, m in quad(lo, hi):
                lifted, near = self.near(self.PR, i, j, m)
                q = self.Q[i, pl.ds(j, m)] - self.D[i, pl.ds(j, m)] * lifted + near
                self.R[i, pl.ds(j, m)] = q
                self.SA[i, pl.ds(j, m)] = q * self.I[i, pl.ds(j, m)] * (1.0 / MID)

        loop(lo, hi, body)


def halo_copies(ref, own, halo, cut, gx, gy, send, recv, first):
    copies = []
    for k, (dx, dy) in enumerate(SIDES):
        src, dst = [], []
        for d, o, h, w in ((dx, own[0], halo[0], cut[0]), (dy, own[1], halo[1], cut[1])):
            if d == 0:
                src.append(pl.ds(h, o))
                dst.append(pl.ds(h, o))
            elif d < 0:
                src.append(pl.ds(h, w))
                dst.append(pl.ds(h + o, w))
            else:
                src.append(pl.ds(h + o - w, w))
                dst.append(pl.ds(h - w, w))
        target = (lax.rem(gx + dx + NX, NX), lax.rem(gy + dy + NY, NY))
        copies.append(
            pltpu.make_async_remote_copy(
                src_ref=ref.at[src[0], src[1]],
                dst_ref=ref.at[dst[0], dst[1]],
                send_sem=send.at[first + k],
                recv_sem=recv.at[first + k],
                device_id=target,
                device_id_type=MESH,
            )
        )
    return copies


def kernel(
    force, phase, table, kinds, out_w, out_r,
    PH, RP1, VP1, QP1, XP1, RP2, VP2, QP2, XP2, MSG, CG, CR, CV, KXM, KXP, KA, KB, KZ, CD, CI, CS, CE, OW, *rest,
):
    refs0, refs1, refs2 = rest[0:12], rest[12:24], rest[24:36]
    in_sem, send, recv = rest[36:]
    gx, gy = lax.axis_index("gx"), lax.axis_index("gy")
    core = lax.rem(gx, 2)
    pair = gx // 2
    L0, L1, L2 = Level(0, 16, 3, refs0), Level(1, 8, 4, refs1), Level(2, 4, 4, refs2)
    group, side, lane = subs() // 2, subs() % 2, lanes()

    loads = []
    for c in range(3):
        for s in range(2):
            loads.append(
                pltpu.make_async_copy(
                    force.at[c, :, :, pl.ds(128 * s, 128)],
                    L0.R.at[pl.ds(3, 16), pl.ds(3, 16), 2 * c + s],
                    in_sem.at[len(loads)],
                )
            )
    for c in range(4):
        for s in range(2):
            loads.append(
                pltpu.make_async_copy(
                    phase.at[:, :, pl.ds(128 * s, 128)], PH.at[:, :, 2 * c + s], in_sem.at[len(loads)]
                )
            )
    for copy in loads:
        copy.start()

    partners = [(lax.rem(gx + dx + NX, NX), lax.rem(gy + dy + NY, NY)) for dx, dy in SIDES]
    partners += [(gx, lax.rem(gy + k, NY)) for k in range(2, 7)]
    partners += [(lax.rem(gx + 2 * k, NX), gy) for k in range(1, 16)]
    barrier = pltpu.get_barrier_semaphore()
    for partner in partners:
        pl.semaphore_signal(barrier, inc=1, device_id=partner, device_id_type=MESH)

    values = jnp.zeros((8, 128), F32)
    for k in range(8):
        values = jnp.where(lane == k, table[k], values)
    for copy in loads:
        copy.wait()

    def look_up(i):
        for j, m in quad(0, 16):
            index = PH[i, pl.ds(j, m)]
            cells = pick_lane(jnp.broadcast_to(values, index.shape), index)
            L0.V[i + 3, pl.ds(j + 3, m)] = cells
            L0.R[i + 3, pl.ds(j + 3, m)] = choose(group == 3, cells, L0.R[i + 3, pl.ds(j + 3, m)])

    loop(0, 16, look_up)
    pl.semaphore_wait(barrier, len(partners))

    pending = halo_copies(L0.R, (16, 16), (3, 3), (2, 2), gx, gy, send, recv, 0)
    for k, (dx, dy) in enumerate(((-1, 0), (1, 0), (0, -1), (0, 1))):
        span = {0: (pl.ds(3, 16), pl.ds(3, 16)), -1: (pl.ds(5, 1), pl.ds(21, 1)), 1: (pl.ds(16, 1), pl.ds(0, 1))}
        pending.append(
            pltpu.make_async_remote_copy(
                src_ref=L0.R.at[span[dx][0], span[dy][0], pl.ds(6, 2)],
                dst_ref=L0.R.at[span[dx][1], span[dy][1], pl.ds(6, 2)],
                send_sem=send.at[8 + k],
                recv_sem=recv.at[8 + k],
                device_id=(lax.rem(gx + dx + NX, NX), lax.rem(gy + dy + NY, NY)),
                device_id_type=MESH,
            )
        )
    for copy in pending:
        copy.start()
    faces = pending
    sent = []

    def restrict(src, halo_src, count, reach, i):
        row = src[halo_src + 2 * i, pl.ds(halo_src, count)] + src[halo_src + 2 * i + 1, pl.ds(halo_src, count)]
        row = row.reshape(count // 2, 2, 8, 128)
        return pair_sum(row[:, 0] + row[:, 1], reach) * 0.125

    def coarsen_v1(i):
        L1.V[4 + i, pl.ds(4, 8)] = restrict(L0.V, 3, 16, 1, i)

    def coarsen_v2(i):
        L2.V[4 + i, pl.ds(4, 4)] = restrict(L1.V, 4, 8, 2, i)

    loop(0, 8, coarsen_v1)
    loop(0, 4, coarsen_v2)

    def pack_v1(a):
        for b in range(2):
            parts = [by_group([L1.V[4 + 2 * a + p, 4 + 4 * b + k] for k in range(4)]) for p in range(2)]
            VP1[a + 2, b + 1] = jnp.where(lane % 2 == 0, parts[0], parts[1])

    loop(0, 4, pack_v1)
    tile = None
    for p in range(4):
        part = by_group([L2.V[4 + p, 4 + k] for k in range(4)])
        tile = part if tile is None else jnp.where(lane % 4 == p, part, tile)
    VP2[1, 1] = tile

    for copy in pending:
        copy.wait_recv()

    early = halo_copies(VP1, (4, 2), (2, 1), (2, 1), gx, gy, send, recv, 12)
    early += halo_copies(VP2, (1, 1), (1, 1), (1, 1), gx, gy, send, recv, 20)
    for copy in early:
        copy.start()
    sent += early

    def fill_v0(i):
        for j, m in quad(0, 22):
            L0.V[i, pl.ds(j, m)] = spread_sub(L0.R[i, pl.ds(j, m)], 3)

    loop(0, 22, fill_v0)
    L0.build(gx, gy, kinds, 1, 21)
    L0.descend()
    for copy in faces:
        copy.wait_send()

    def pack_r1(a):
        one, other = restrict(L0.Q, 3, 16, 1, 2 * a), restrict(L0.Q, 3, 16, 1, 2 * a + 1)
        RP1[a + 1, pl.ds(2, 8)] = choose(lane % 2 == 0, one, other)

    loop(0, 4, pack_r1)
    pending = halo_copies(RP1, (4, 8), (1, 2), (1, 2), gx, gy, send, recv, 28)
    for copy in pending:
        copy.start()
    sent += pending
    for copy in early:
        copy.wait_recv()

    def unpack_v1(a):
        for b in range(4):
            both = VP1[a, b]
            for p in range(2):
                part = pick_lane(both, (lane // 2) * 2 + p)
                for k in range(4):
                    L1.V[2 * a + p, 4 * b + k] = spread_sub(part, k)

    loop(0, 8, unpack_v1)

    def unpack_v2(a):
        for b in range(3):
            both = VP2[a, b]
            for p in range(4):
                part = pick_lane(both, (lane // 4) * 4 + p)
                for k in range(4):
                    L2.V[4 * a + p, 4 * b + k] = spread_sub(part, k)

    loop(0, 3, unpack_v2)
    L1.build(gx, gy, kinds, 1, 15)
    L2.build(gx, gy, kinds, 1, 11)
    for copy in pending:
        copy.wait_recv()

    def unpack_pairs(src, dst, count, x_first, y_first, y_count):
        def body(a):
            row = src[a, pl.ds(0, y_count)]
            for p in range(2):
                dst[x_first + 2 * a + p, pl.ds(y_first, y_count)] = pick_lane(row, (lane // 2) * 2 + p)

        loop(0, count, body)

    unpack_pairs(RP1, L1.R, 6, 2, 2, 12)
    L1.descend()

    def pack_r2(a):
        rows = []
        for p in range(2):
            row = restrict(L1.Q, 4, 8, 2, 2 * a + p).reshape(2, 2, 8, 128)
            rows.append(choose(lane % 2 == 0, row[:, 0], row[:, 1]))
        RP2[a + 1, pl.ds(1, 2)] = choose(lane % 4 < 2, rows[0], rows[1])

    loop(0, 2, pack_r2)
    pending = halo_copies(RP2, (2, 2), (1, 1), (1, 1), gx, gy, send, recv, 36)
    for copy in pending:
        copy.start()
    sent += pending
    for copy in pending:
        copy.wait_recv()

    def unpack_quads(src, dst, count, first):
        def body(a):
            for b in range(count):
                both = src[a, b]
                for p in range(2):
                    for k in range(2):
                        dst[first + 2 * a + p, first + 2 * b + k] = pick_lane(both, (lane // 4) * 4 + (2 * p + k))

        loop(0, count, body)

    unpack_quads(RP2, L2.R, 4, 2)
    L2.descend()

    for p in range(2):
        r3 = restrict(L2.Q, 4, 4, 4, p)
        v3 = restrict(L2.V, 4, 4, 4, p)
        both = choose(group == 3, v3, r3)
        both = pick_lane(both, 8 * (lane % 16))
        both = jnp.where(tiled(lane // 16 == subs(), both), both, 0.0)
        for k in range(2):
            MSG[pl.ds(2 * p + k, 1), :] = jnp.sum(both[k], axis=0, keepdims=True)
    rows = pl.ds(pl.multiple_of(4 * gy, 4), 4)
    keep = pltpu.make_async_copy(MSG.at[pl.ds(0, 4)], CG.at[pair, core, rows], in_sem.at[0])
    keep.start()
    pending = []
    for k in range(1, 16):
        pending.append(
            pltpu.make_async_remote_copy(
                src_ref=MSG.at[pl.ds(0, 4)],
                dst_ref=CG.at[pair, core, rows],
                send_sem=send.at[44 + k - 1],
                recv_sem=recv.at[44 + k - 1],
                device_id=(lax.rem(gx + 2 * k, NX), gy),
                device_id_type=MESH,
            )
        )
    for copy in pending:
        copy.start()
    sent += pending

    def pack_1(a):
        for src, dst, x0, y0 in ((L1.Q, QP1, 2, 3), (L1.X, XP1, 1, 2)):
            one, other = src[4 + 2 * a, pl.ds(4, 8)], src[5 + 2 * a, pl.ds(4, 8)]
            dst[x0 + a, pl.ds(y0, 8)] = choose(lane % 2 == 0, one, other)

    loop(0, 4, pack_1)

    def pack_2(a):
        for src, dst, x0 in ((L2.Q, QP2, 2), (L2.X, XP2, 1)):
            mixed = []
            for p in range(2):
                row = src[4 + 2 * a + p, pl.ds(4, 4)].reshape(2, 2, 8, 128)
                mixed.append(choose(lane % 2 == 0, row[:, 0], row[:, 1]))
            dst[x0 + a, pl.ds(x0, 2)] = choose(lane % 4 < 2, mixed[0], mixed[1])

    loop(0, 2, pack_2)
    keep.wait()
    for copy in pending:
        copy.wait_recv()

    pending = []
    for k in range(1, 8):
        pending.append(
            pltpu.make_async_remote_copy(
                src_ref=CG.at[:, core, rows],
                dst_ref=CG.at[:, core, rows],
                send_sem=send.at[59 + k - 1],
                recv_sem=recv.at[59 + k - 1],
                device_id=(gx, lax.rem(gy + k, NY)),
                device_id_type=MESH,
            )
        )
    for copy in pending:
        copy.start()
    sent += pending
    for copy in pending:
        copy.wait_recv()
    swap = pltpu.make_async_remote_copy(
        src_ref=CG.at[:, core],
        dst_ref=CG.at[:, core],
        send_sem=send.at[66],
        recv_sem=recv.at[66],
        device_id=(gx + 1 - 2 * core, gy),
        device_id_type=MESH,
    )
    swap.start()
    sent.append(swap)
    late2 = halo_copies(QP2, (2, 2), (2, 2), (2, 2), gx, gy, send, recv, 67)
    late2 += halo_copies(XP2, (2, 2), (1, 1), (1, 1), gx, gy, send, recv, 75)
    late1 = halo_copies(QP1, (4, 8), (2, 3), (2, 3), gx, gy, send, recv, 83)
    late1 += halo_copies(XP1, (4, 8), (1, 2), (1, 2), gx, gy, send, recv, 91)
    late0 = halo_copies(L0.Q, (16, 16), (3, 3), (2, 2), gx, gy, send, recv, 99)
    swap.wait_recv()
    for copy in late2 + late1 + late0:
        copy.start()
    sent += late2 + late1 + late0

    coarse(gx, gy, kinds, CG, CR, CV, KXM, KXP, KA, KB, KZ, CD, CI, CS, CE)

    flat = CE.reshape(96, 128)

    def expand(a):
        for j in range(6):
            row = 16 * a + 8 * (j % 2) + lax.rem(gy + 7 + j // 2, 8)
            both = jnp.broadcast_to(flat[pl.ds(row, 1), :], (8, 128))
            both = pick_lane(both, 16 * subs() + lane // 8)
            for p in range(2):
                for k in range(2):
                    L2.PR[2 * a + p, 2 * j + k] = both

    loop(0, 6, expand)

    for copy in late2:
        copy.wait_recv()
    unpack_quads(QP2, L2.Q, 6, 0)
    unpack_quads(XP2, L2.X, 4, 2)

    def middle(level):
        h, b = level.halo, level.block
        level.correct(h - 3, h + b + 3)
        level.second_step(level.R, level.R, h - 2, h + b + 2)

        def body(i):
            for j, m in quad(h - 2, h + b + 2):
                here = pl.ds(j, m)
                level.SB[i, here] = (level.X[i, here] + level.PR[i, here]) + (level.SA[i, here] + level.SB[i, here])

        loop(h - 2, h + b + 2, body)

    middle(L2)
    L1.lift(L2.SB, (0, 2), 2, 8)
    for copy in late1:
        copy.wait_recv()

    def unpack_q1(a):
        row = QP1[a]
        for p in range(2):
            L1.Q[2 * a + p, pl.ds(1, 14)] = pick_lane(row, (lane // 2) * 2 + p)

    loop(0, 8, unpack_q1)
    unpack_pairs(XP1, L1.X, 6, 2, 2, 12)
    middle(L1)
    L0.lift(L1.SB, (1, 2), 2, 12)
    for copy in late0:
        copy.wait_recv()
    L0.correct(1, 21)
    L0.second_step(L0.R, L0.R, 2, 20)

    def last(i):
        for j, m in quad(3, 19):
            here = pl.ds(j, m)
            step, near = L0.near(L0.SB, i, j, m)
            diag = L0.D[i, here]
            field = (L0.X[i, here] + L0.PR[i, here]) + (L0.SA[i, here] + step)
            L0.R[i, here] = L0.R[i, here] - diag * step + near
            OW[i - 3, pl.ds(j - 3, m)] = diag * field

    loop(3, 19, last)
    stores = []
    for c in range(3):
        for s in range(2):
            place = pl.ds(128 * s, 128)
            stores.append(
                pltpu.make_async_copy(OW.at[:, :, 2 * c + s], out_w.at[c, :, :, place], in_sem.at[len(stores)])
            )
            stores.append(
                pltpu.make_async_copy(
                    L0.R.at[pl.ds(3, 16), pl.ds(3, 16), 2 * c + s],
                    out_r.at[c, :, :, place],
                    in_sem.at[len(stores)],
                )
            )
    for copy in stores:
        copy.start()
    for copy in sent:
        copy.wait_send()
    for copy in stores:
        copy.wait()


def coarse(gx, gy, kinds, CG, CR, CV, KXM, KXP, KA, KB, KZ, CD, CI, CS, CE):
    planes = 2 * NX
    scale = 0.25 ** (LEVELS - 1)
    lane = lanes()
    spot = lane % 32
    flat = CG.reshape(1024, 128)

    def blocks(reach, body):
        lo = jnp.maximum(2 * gx - 2 - reach, 0) // BLOCK
        hi = (jnp.minimum(2 * gx + 4 + reach, planes) + BLOCK - 1) // BLOCK
        loop(lo, hi, body)

    zeros = jnp.zeros((PAD, 2, 8, 128), F32)
    for place in (0, PAD + planes):
        CV[pl.ds(place, PAD)] = zeros
        CS[0, pl.ds(place, PAD)] = zeros
        CS[1, pl.ds(place, PAD)] = zeros

    def take(b):
        for q in range(BLOCK):
            for y in range(2):
                start = 128 * b // 2 + 32 * (q // 2) + 2 * (q % 2) + y
                row = flat[pl.ds(start, 8, stride=4), :]
                CR[PAD + BLOCK * b + q, y] = row
                CV[PAD + BLOCK * b + q, y] = pick_lane(row, 96 + spot)

    blocks(26, take)

    def per_kind(wall):
        tile = jnp.zeros((8, 128), F32)
        for c in range(3):
            tile = jnp.where(lane // 32 == c, kinds[c, wall].astype(F32), tile)
        return tile

    walls = [per_kind(wall) for wall in range(6)]
    z_wall = jnp.where(spot == 0, walls[4], 0.0) + jnp.where(spot == 31, walls[5], 0.0)
    low_y = z_wall + jnp.where(subs() == 0, walls[2], 0.0)
    high_y = z_wall + jnp.where(subs() == 7, walls[3], 0.0)

    def setup(b):
        here = pl.ds(PAD + BLOCK * b, BLOCK)
        prev, after = pl.ds(PAD - 1 + BLOCK * b, BLOCK), pl.ds(PAD + 1 + BLOCK * b, BLOCK)
        plane = lax.broadcasted_iota(jnp.int32, (BLOCK, 8, 128), 0) + BLOCK * b
        even, odd = CV[here, 0], CV[here, 1]
        half = 0.5 * scale
        ka = half * (even + odd)
        kb = half * (odd + roll_sub(even, -1))
        kb = jnp.where(tiled(subs() == 7, kb), 0.0, kb)
        KA[here] = ka
        KB[here] = kb
        x_wall = jnp.where(plane == 0, tiled(walls[0], even), 0.0)
        x_wall = x_wall + jnp.where(plane == planes - 1, tiled(walls[1], even), 0.0)
        for y, value, wall, other in ((0, even, low_y, roll_sub(kb, 1)), (1, odd, high_y, kb)):
            kxm = jnp.where(plane == 0, 0.0, half * (CV[prev, y] + value))
            kxp = jnp.where(plane == planes - 1, 0.0, half * (value + CV[after, y]))
            kz = half * (value + roll_lane(value, -1))
            kz = jnp.where(tiled(spot == 31, kz), 0.0, kz)
            KXM[here, y] = kxm
            KXP[here, y] = kxp
            KZ[here, y] = kz
            total = (kxm + kxp) + (ka + other) + (kz + roll_lane(kz, 1))
            total = total + (2.0 * scale) * value * (x_wall + tiled(wall, value))
            CD[here, y] = total
            inverse = 1.0 / total
            CI[here, y] = inverse
            CS[0, here, y] = CR[here, y] * inverse * (1.0 / CMID)

    blocks(25, setup)

    own = pl.ds(PAD - 2 + 2 * gx, 6)
    CE[...] = CS[0, own]

    def sweep(k, rho):
        now, later = lax.rem(k, 2), lax.rem(k + 1, 2)
        rho_next = 1.0 / (2.0 * CSIG - rho)
        step_a = rho_next * rho
        step_b = rho_next * (2.0 / CRAD)

        def body(b):
            here = pl.ds(PAD + BLOCK * b, BLOCK)
            prev, after = pl.ds(PAD - 1 + BLOCK * b, BLOCK), pl.ds(PAD + 1 + BLOCK * b, BLOCK)
            even, odd = CS[now, here, 0], CS[now, here, 1]
            ka, kb = KA[here], KB[here]
            for y, value, beside in (
                (0, even, ka * odd + roll_sub(kb * odd, 1)),
                (1, odd, ka * even + kb * roll_sub(even, -1)),
            ):
                kz = KZ[here, y]
                near = KXM[here, y] * CS[now, prev, y] + KXP[here, y] * CS[now, after, y] + beside
                near = near + (kz * roll_lane(value, -1) + roll_lane(kz * value, 1))
                r = CR[here, y] - CD[here, y] * value + near
                CR[here, y] = r
                CS[later, here, y] = tiled(step_a, r) * value + tiled(step_b, r) * (r * CI[here, y])

        blocks(CSWEEPS - 2 - k, body)
        CE[...] = CE[...] + CS[later, own]
        return rho_next

    lax.fori_loop(0, CSWEEPS - 1, sweep, jnp.full((8, 128), 1.0 / CSIG, F32))


def per_device(body_force, phase, viscosity_table, wall_kinds):
    def vmem(*lead):
        return pltpu.VMEM(lead + (8, 128), F32)

    scratch = [
        pltpu.VMEM((16, 16, 8, 128), jnp.int32),
        vmem(6, 12), vmem(8, 4), vmem(8, 14), vmem(6, 12),
        vmem(4, 4), vmem(3, 3), vmem(6, 6), vmem(4, 4),
        vmem(), pltpu.VMEM((16, 2, 32, 128), F32),
    ]
    depth = 2 * NX + 2 * PAD
    scratch += [vmem(depth, 2)] * 4 + [vmem(depth)] * 2 + [vmem(depth, 2)] * 3 + [vmem(2, depth, 2), vmem(6, 2)]
    scratch += [vmem(16, 16)]
    for frame in (22, 16, 12):
        scratch += [vmem(frame, frame)] * 12
    n_sems = 107
    scratch += [pltpu.SemaphoreType.DMA((14,)), pltpu.SemaphoreType.DMA((n_sems,)), pltpu.SemaphoreType.DMA((n_sems,))]
    shape = jax.ShapeDtypeStruct(body_force.shape, F32)
    return pl.pallas_call(
        kernel,
        out_shape=(shape, shape),
        in_specs=[
            pl.BlockSpec(memory_space=pl.ANY),
            pl.BlockSpec(memory_space=pl.ANY),
            pl.BlockSpec(memory_space=pltpu.SMEM),
            pl.BlockSpec(memory_space=pltpu.SMEM),
        ],
        out_specs=(pl.BlockSpec(memory_space=pl.ANY), pl.BlockSpec(memory_space=pl.ANY)),
        scratch_shapes=scratch,
        compiler_params=pltpu.CompilerParams(
            collective_id=0, has_side_effects=True, vmem_limit_bytes=56 * 2**20
        ),
        name="vcycle",
    )(body_force, phase, viscosity_table, wall_kinds)


def solution(mesh):
    placed = (P(None, "gx", "gy", None), P("gx", "gy", None), P(), P())
    return jax.shard_map(
        per_device,
        mesh=mesh,
        in_specs=placed,
        out_specs=(P(None, "gx", "gy", None), P(None, "gx", "gy", None)),
        check_vma=False,
    )
```

time: 846 us -> 99.1 us (0.12)
  the two profiles are of different devices: /device:TPU:2 before, /device:TPU:3 now
where the time goes in v1:
time: 99.1 us; the launch traced here: 98.9 us
  Pallas kernels  95.2 us (96%)
  local copies, waits for them, and re-layouts  3.02 us (3%)
    pallas_call x1, Pallas kernels, per_device(): pl.pallas_call(kernel, out_shape=(shape, shape), in_specs=[pl.BlockSpec(m...  95.2 us
    unnamed x4, local copies, waits for them, and re-layouts  3.02 us

profile of v1, /device:TPU:3, one launch (start us, length us, event | category | flops | bytes accessed | tf_op | source)
XLA Modules:
  0.0 98.9 jit_solution(9369263955773263903)
XLA Ops:
  0.6 95.2 %vcycle.1 = (f32[3,16,16,256]{3,2,1,0:T(8,128)}, f32[3,16,16,256]{3,2,1,0:T(8,128)}) custom-call(f32[3,16,16,256]{3,2,1,0:T(8,128)} %force.1, s32[16,16,256]{2,1,0:T(8,128)} %phase.1, f32[8]{0:T(128)} %table.1, s32[3,6]{1,0:T(4,128)} %kinds.1), custom_call_target="tpu_custom_call" | custom-call | tf_op jit(solution)/shard_map/vcycle/pallas_call | solution.py:731
  95.9 0.0 copy-start
  95.9 2.1 %copy.8 = f32[3,16,16,256]{3,2,1,0:T(8,128)} copy(f32[3,16,16,256]{3,2,1,0:T(8,128)} %get-tuple-element.4) | data formatting | bytes 1572864
  98.0 0.0 copy-done
  98.0 0.9 copy.9
Async XLA Ops:
  95.9 2.1 %copy-start = (f32[3,16,16,256]{3,2,1,0:T(8,128)S(1)}, f32[3,16,16,256]{3,2,1,0:T(8,128)}, u32[]{:S(2)}) copy-start(f32[3,16,16,256]{3,2,1,0:T(8,128)} %get-tuple-element.5) | copy-start | bytes 2359300

commit v2 on v1

--- a/solution.py
+++ b/solution.py
@@ -29,7 +29,7 @@
 
 SIDES = [(dx, dy) for dx in (-1, 0, 1) for dy in (-1, 0, 1) if dx or dy]
 PAD = 4
-BLOCK = 4
+BLOCK = 16
 CHUNK = 8
 
 
@@ -94,11 +94,24 @@
 
 
 def loop(lo, hi, body):
-    def step(i, carry):
-        body(i)
+    whole = isinstance(lo, int) and isinstance(hi, int)
+    turns = next(k for k in (4, 3, 2, 1) if k == 1 or whole and (hi - lo) % k == 0)
+
+    def step(t, carry):
+        for k in range(turns):
+            body(lo + turns * t + k)
         return carry
 
-    lax.fori_loop(lo, hi, step, 0)
+    lax.fori_loop(0, (hi - lo) // turns, step, 0)
+
+
+def clear(ref):
+    rows, columns = ref.shape[:2]
+
+    def body(i):
+        ref[i] = jnp.zeros((columns, 8, 128), F32)
+
+    loop(0, rows, body)
 
 
 class Level:
@@ -221,11 +234,12 @@
         loop(lo, hi, body)
 
 
-def halo_copies(ref, own, halo, cut, gx, gy, send, recv, first):
+def halo_copies(ref, own, halo, cut, corner, gx, gy, send, recv, first, height=6):
     copies = []
     for k, (dx, dy) in enumerate(SIDES):
         src, dst = [], []
-        for d, o, h, w in ((dx, own[0], halo[0], cut[0]), (dy, own[1], halo[1], cut[1])):
+        wide = corner if dx and dy else cut
+        for d, o, h, w in ((dx, own[0], halo[0], wide[0]), (dy, own[1], halo[1], wide[1])):
             if d == 0:
                 src.append(pl.ds(h, o))
                 dst.append(pl.ds(h, o))
@@ -238,8 +252,8 @@
         target = (lax.rem(gx + dx + NX, NX), lax.rem(gy + dy + NY, NY))
         copies.append(
             pltpu.make_async_remote_copy(
-                src_ref=ref.at[src[0], src[1]],
-                dst_ref=ref.at[dst[0], dst[1]],
+                src_ref=ref.at[src[0], src[1], pl.ds(0, height)],
+                dst_ref=ref.at[dst[0], dst[1], pl.ds(0, height)],
                 send_sem=send.at[first + k],
                 recv_sem=recv.at[first + k],
                 device_id=target,
@@ -281,6 +295,9 @@
     for copy in loads:
         copy.start()
 
+    for ref in (RP1, QP1, XP1, RP2, QP2, XP2, L0.Q):
+        clear(ref)
+
     partners = [(lax.rem(gx + dx + NX, NX), lax.rem(gy + dy + NY, NY)) for dx, dy in SIDES]
     partners += [(gx, lax.rem(gy + k, NY)) for k in range(2, 7)]
     partners += [(lax.rem(gx + 2 * k, NX), gy) for k in range(1, 16)]
@@ -304,7 +321,7 @@
     loop(0, 16, look_up)
     pl.semaphore_wait(barrier, len(partners))
 
-    pending = halo_copies(L0.R, (16, 16), (3, 3), (2, 2), gx, gy, send, recv, 0)
+    pending = halo_copies(L0.R, (16, 16), (3, 3), (2, 2), (2, 2), gx, gy, send, recv, 0, 8)
     for k, (dx, dy) in enumerate(((-1, 0), (1, 0), (0, -1), (0, 1))):
         span = {0: (pl.ds(3, 16), pl.ds(3, 16)), -1: (pl.ds(5, 1), pl.ds(21, 1)), 1: (pl.ds(16, 1), pl.ds(0, 1))}
         pending.append(
@@ -351,8 +368,8 @@
     for copy in pending:
         copy.wait_recv()
 
-    early = halo_copies(VP1, (4, 2), (2, 1), (2, 1), gx, gy, send, recv, 12)
-    early += halo_copies(VP2, (1, 1), (1, 1), (1, 1), gx, gy, send, recv, 20)
+    early = halo_copies(VP1, (4, 2), (2, 1), (2, 1), (2, 1), gx, gy, send, recv, 12, 8)
+    early += halo_copies(VP2, (1, 1), (1, 1), (1, 1), (1, 1), gx, gy, send, recv, 20, 8)
     for copy in early:
         copy.start()
     sent += early
@@ -372,7 +389,7 @@
         RP1[a + 1, pl.ds(2, 8)] = choose(lane % 2 == 0, one, other)
 
     loop(0, 4, pack_r1)
-    pending = halo_copies(RP1, (4, 8), (1, 2), (1, 2), gx, gy, send, recv, 28)
+    pending = halo_copies(RP1, (4, 8), (1, 2), (1, 2), (1, 1), gx, gy, send, recv, 28)
     for copy in pending:
         copy.start()
     sent += pending
@@ -422,10 +439,14 @@
         RP2[a + 1, pl.ds(1, 2)] = choose(lane % 4 < 2, rows[0], rows[1])
 
     loop(0, 2, pack_r2)
-    pending = halo_copies(RP2, (2, 2), (1, 1), (1, 1), gx, gy, send, recv, 36)
+    pending = halo_copies(RP2, (2, 2), (1, 1), (1, 1), (1, 1), gx, gy, send, recv, 36)
     for copy in pending:
         copy.start()
     sent += pending
+    late0 = halo_copies(L0.Q, (16, 16), (3, 3), (2, 2), (1, 1), gx, gy, send, recv, 99)
+    for copy in late0:
+        copy.start()
+    sent += late0
     for copy in pending:
         copy.wait_recv()
 
@@ -485,6 +506,13 @@
             dst[x0 + a, pl.ds(x0, 2)] = choose(lane % 4 < 2, mixed[0], mixed[1])
 
     loop(0, 2, pack_2)
+    late2 = halo_copies(QP2, (2, 2), (2, 2), (2, 2), (2, 2), gx, gy, send, recv, 67)
+    late2 += halo_copies(XP2, (2, 2), (1, 1), (1, 1), (1, 1), gx, gy, send, recv, 75)
+    late1 = halo_copies(QP1, (4, 8), (2, 3), (2, 3), (1, 2), gx, gy, send, recv, 83)
+    late1 += halo_copies(XP1, (4, 8), (1, 2), (1, 2), (1, 1), gx, gy, send, recv, 91)
+    for copy in late2 + late1:
+        copy.start()
+    sent += late2 + late1
     keep.wait()
     for copy in pending:
         copy.wait_recv()
@@ -516,15 +544,7 @@
     )
     swap.start()
     sent.append(swap)
-    late2 = halo_copies(QP2, (2, 2), (2, 2), (2, 2), gx, gy, send, recv, 67)
-    late2 += halo_copies(XP2, (2, 2), (1, 1), (1, 1), gx, gy, send, recv, 75)
-    late1 = halo_copies(QP1, (4, 8), (2, 3), (2, 3), gx, gy, send, recv, 83)
-    late1 += halo_copies(XP1, (4, 8), (1, 2), (1, 2), gx, gy, send, recv, 91)
-    late0 = halo_copies(L0.Q, (16, 16), (3, 3), (2, 2), gx, gy, send, recv, 99)
     swap.wait_recv()
-    for copy in late2 + late1 + late0:
-        copy.start()
-    sent += late2 + late1 + late0
 
     coarse(gx, gy, kinds, CG, CR, CV, KXM, KXP, KA, KB, KZ, CD, CI, CS, CE)
 
@@ -630,7 +650,7 @@
     def take(b):
         for q in range(BLOCK):
             for y in range(2):
-                start = 128 * b // 2 + 32 * (q // 2) + 2 * (q % 2) + y
+                start = 16 * BLOCK * b + 32 * (q // 2) + 2 * (q % 2) + y
                 row = flat[pl.ds(start, 8, stride=4), :]
                 CR[PAD + BLOCK * b + q, y] = row
                 CV[PAD + BLOCK * b + q, y] = pick_lane(row, 96 + spot)

time: 99.1 us -> 80.4 us (0.81)
  Pallas kernels: 95.2 us -> 76.6 us
    pallas_call x1, Pallas kernels: 95.2 us -> 76.6 us  [per_device(): pl.pallas_call(kernel, out_shape=(shape, shape), in_specs=[pl.BlockSpec(m...]
where the time goes in v2:
time: 80.4 us; the launch traced here: 80.3 us
  Pallas kernels  76.6 us (95%)
  local copies, waits for them, and re-layouts  3.02 us (4%)
    pallas_call x1, Pallas kernels, per_device(): pl.pallas_call(kernel, out_shape=(shape, shape), in_specs=[pl.BlockSpec(m...  76.6 us
    unnamed x4, local copies, waits for them, and re-layouts  3.02 us

profile of v2, /device:TPU:3, one launch (start us, length us, event | category | flops | bytes accessed | tf_op | source)
XLA Modules:
  0.0 80.3 jit_solution(14675081095804654816)
XLA Ops:
  0.6 76.6 %vcycle.1 = (f32[3,16,16,256]{3,2,1,0:T(8,128)}, f32[3,16,16,256]{3,2,1,0:T(8,128)}) custom-call(f32[3,16,16,256]{3,2,1,0:T(8,128)} %force.1, s32[16,16,256]{2,1,0:T(8,128)} %phase.1, f32[8]{0:T(128)} %table.1, s32[3,6]{1,0:T(4,128)} %kinds.1), custom_call_target="tpu_custom_call" | custom-call | tf_op jit(solution)/shard_map/vcycle/pallas_call | solution.py:751
  77.3 0.0 copy-start
  77.3 2.1 %copy.8 = f32[3,16,16,256]{3,2,1,0:T(8,128)} copy(f32[3,16,16,256]{3,2,1,0:T(8,128)} %get-tuple-element.4) | data formatting | bytes 1572864
  79.4 0.0 copy-done
  79.4 0.9 %copy.9 = f32[3,16,16,256]{3,2,1,0:T(8,128)} copy(f32[3,16,16,256]{3,2,1,0:T(8,128)S(1)} %copy-done) | data formatting | bytes 1572864
Async XLA Ops:
  77.3 2.1 %copy-start = (f32[3,16,16,256]{3,2,1,0:T(8,128)S(1)}, f32[3,16,16,256]{3,2,1,0:T(8,128)}, u32[]{:S(2)}) copy-start(f32[3,16,16,256]{3,2,1,0:T(8,128)} %get-tuple-element.5) | copy-start | bytes 2359300

commit v3 on v2

--- a/solution.py
+++ b/solution.py
@@ -30,6 +30,7 @@
 SIDES = [(dx, dy) for dx in (-1, 0, 1) for dy in (-1, 0, 1) if dx or dy]
 PAD = 4
 BLOCK = 16
+PLANES = 8
 CHUNK = 8
 
 
@@ -93,9 +94,10 @@
     return [(j, min(CHUNK, hi - j)) for j in range(lo, hi, CHUNK)]
 
 
-def loop(lo, hi, body):
+def loop(lo, hi, body, width=CHUNK):
     whole = isinstance(lo, int) and isinstance(hi, int)
-    turns = next(k for k in (4, 3, 2, 1) if k == 1 or whole and (hi - lo) % k == 0)
+    most = 7 if width <= 4 else 4
+    turns = next(k for k in range(most, 0, -1) if k == 1 or whole and (hi - lo) % k == 0)
 
     def step(t, carry):
         for k in range(turns):
@@ -133,7 +135,7 @@
         out = out + (kz * above(mid, self.reach) + below(kz * mid, self.reach))
         return mid, out
 
-    def build(self, gx, gy, kinds, lo, hi):
+    def build(self, gx, gy, kinds, top, bottom, lo, hi):
         h, b = self.halo, self.block
         half = 0.5 * self.scale
         group, side = subs() // 2, subs() % 2
@@ -159,15 +161,16 @@
                 here = self.V[i, pl.ds(j, m)]
                 self.KX[i, pl.ds(j, m)] = (half * open_x) * (self.V[i - 1, pl.ds(j, m)] + here)
 
-        loop(lo, hi + 1, faces)
+        loop(top, bottom + 1, faces, hi - lo)
 
         def rest(i):
             x_wall = z_wall + jnp.where(i == h, at_x[0], zero) * walls[0]
             x_wall = x_wall + jnp.where(i == h + b - 1, at_x[1], zero) * walls[1]
             for j, m in quad(lo, hi + 1):
                 self.KY[i, pl.ds(j, m)] = half * (self.V[i, pl.ds(j - 1, m)] + self.V[i, pl.ds(j, m)])
-            self.KY[i, h] = self.KY[i, h] * (one - at_y[0])
-            self.KY[i, h + b] = self.KY[i, h + b] * (one - at_y[1])
+            for j, at in ((h, at_y[0]), (h + b, at_y[1])):
+                if lo <= j <= hi:
+                    self.KY[i, j] = self.KY[i, j] * (one - at)
             for j, m in quad(lo, hi):
                 here = self.V[i, pl.ds(j, m)]
                 ky = self.KY[i, pl.ds(j, m + 1)]
@@ -178,20 +181,21 @@
                 total = total + (kz + below(kz, self.reach))
                 self.D[i, pl.ds(j, m)] = total + (2.0 * self.scale) * here * tiled(x_wall, here)
             for j, wall, at in ((h, walls[2], at_y[0]), (h + b - 1, walls[3], at_y[1])):
-                self.D[i, j] = self.D[i, j] + (2.0 * self.scale * at) * self.V[i, j] * wall
+                if lo <= j < hi:
+                    self.D[i, j] = self.D[i, j] + (2.0 * self.scale * at) * self.V[i, j] * wall
             for j, m in quad(lo, hi):
                 self.I[i, pl.ds(j, m)] = 1.0 / self.D[i, pl.ds(j, m)]
 
-        loop(lo, hi, rest)
-
-    def first_step(self, src, lo, hi):
+        loop(top, bottom, rest, hi - lo)
+
+    def first_step(self, src, top, bottom, lo, hi):
         def body(i):
             for j, m in quad(lo, hi):
                 self.SA[i, pl.ds(j, m)] = src[i, pl.ds(j, m)] * self.I[i, pl.ds(j, m)] * (1.0 / MID)
 
-        loop(lo, hi, body)
-
-    def second_step(self, src, dst, lo, hi):
+        loop(top, bottom, body, hi - lo)
+
+    def second_step(self, src, dst, top, bottom, lo, hi):
         def body(i):
             for j, m in quad(lo, hi):
                 step, near = self.near(self.SA, i, j, m)
@@ -199,20 +203,26 @@
                 dst[i, pl.ds(j, m)] = r
                 self.SB[i, pl.ds(j, m)] = STEP_A * step + STEP_B * (r * self.I[i, pl.ds(j, m)])
 
-        loop(lo, hi, body)
-
-    def descend(self):
-        h, b = self.halo, self.block
-        self.first_step(self.R, h - 2, h + b + 2)
-        self.second_step(self.R, self.Q, h - 1, h + b + 1)
-
+        loop(top, bottom, body, hi - lo)
+
+    def third_step(self, top, bottom, lo, hi):
         def body(i):
-            for j, m in quad(h, h + b):
+            for j, m in quad(lo, hi):
                 step, near = self.near(self.SB, i, j, m)
                 self.Q[i, pl.ds(j, m)] = self.Q[i, pl.ds(j, m)] - self.D[i, pl.ds(j, m)] * step + near
                 self.X[i, pl.ds(j, m)] = self.SA[i, pl.ds(j, m)] + step
 
-        loop(h, h + b, body)
+        loop(top, bottom, body, hi - lo)
+
+    def descend(self, parts=None):
+        h, e = self.halo, self.halo + self.block
+        parts = parts or (lambda lo, hi, margin: [(lo, hi, lo, hi)])
+        for part in parts(h - 2, e + 2, 1):
+            self.first_step(self.R, *part)
+        for part in parts(h - 1, e + 1, 2):
+            self.second_step(self.R, self.Q, *part)
+        for part in parts(h, e, 3):
+            self.third_step(*part)
 
     def lift(self, ref, shift, first, count):
         def body(i):
@@ -265,7 +275,7 @@
 
 def kernel(
     force, phase, table, kinds, out_w, out_r,
-    PH, RP1, VP1, QP1, XP1, RP2, VP2, QP2, XP2, MSG, CG, CR, CV, KXM, KXP, KA, KB, KZ, CD, CI, CS, CE, OW, *rest,
+    PH, RP1, VP1, QP1, XP1, RP2, VP2, QP2, XP2, MSG, CG, CR, CV, KXM, KXP, KA, KB, KZ, CD, CI, CSA, CSB, CRB, CE, OW, *rest,
 ):
     refs0, refs1, refs2 = rest[0:12], rest[12:24], rest[24:36]
     in_sem, send, recv = rest[36:]
@@ -365,6 +375,16 @@
         tile = part if tile is None else jnp.where(lane % 4 == p, part, tile)
     VP2[1, 1] = tile
 
+    def inside(lo, hi, margin):
+        return [(3 + margin, 19 - margin, 3 + margin, 19 - margin)]
+
+    def around(lo, hi, margin):
+        a, b = 3 + margin, 19 - margin
+        return [(lo, a, lo, hi), (b, hi, lo, hi), (a, b, lo, a), (a, b, b, hi)]
+
+    for part in inside(1, 21, 1):
+        L0.build(gx, gy, kinds, *part)
+    L0.descend(inside)
     for copy in pending:
         copy.wait_recv()
 
@@ -374,13 +394,16 @@
         copy.start()
     sent += early
 
-    def fill_v0(i):
-        for j, m in quad(0, 22):
-            L0.V[i, pl.ds(j, m)] = spread_sub(L0.R[i, pl.ds(j, m)], 3)
-
-    loop(0, 22, fill_v0)
-    L0.build(gx, gy, kinds, 1, 21)
-    L0.descend()
+    for top, bottom, lo, hi in around(0, 22, 0):
+
+        def fill_v0(i):
+            for j, m in quad(lo, hi):
+                L0.V[i, pl.ds(j, m)] = spread_sub(L0.R[i, pl.ds(j, m)], 3)
+
+        loop(top, bottom, fill_v0, hi - lo)
+    for part in around(1, 21, 1):
+        L0.build(gx, gy, kinds, *part)
+    L0.descend(around)
     for copy in faces:
         copy.wait_send()
 
@@ -415,8 +438,8 @@
                     L2.V[4 * a + p, 4 * b + k] = spread_sub(part, k)
 
     loop(0, 3, unpack_v2)
-    L1.build(gx, gy, kinds, 1, 15)
-    L2.build(gx, gy, kinds, 1, 11)
+    L1.build(gx, gy, kinds, 1, 15, 1, 15)
+    L2.build(gx, gy, kinds, 1, 11, 1, 11)
     for copy in pending:
         copy.wait_recv()
 
@@ -510,9 +533,6 @@
     late2 += halo_copies(XP2, (2, 2), (1, 1), (1, 1), (1, 1), gx, gy, send, recv, 75)
     late1 = halo_copies(QP1, (4, 8), (2, 3), (2, 3), (1, 2), gx, gy, send, recv, 83)
     late1 += halo_copies(XP1, (4, 8), (1, 2), (1, 2), (1, 1), gx, gy, send, recv, 91)
-    for copy in late2 + late1:
-        copy.start()
-    sent += late2 + late1
     keep.wait()
     for copy in pending:
         copy.wait_recv()
@@ -544,9 +564,12 @@
     )
     swap.start()
     sent.append(swap)
+    for copy in late2 + late1:
+        copy.start()
+    sent += late2 + late1
     swap.wait_recv()
 
-    coarse(gx, gy, kinds, CG, CR, CV, KXM, KXP, KA, KB, KZ, CD, CI, CS, CE)
+    coarse(gx, gy, kinds, CG, CR, CV, KXM, KXP, KA, KB, KZ, CD, CI, CSA, CSB, CRB, CE)
 
     flat = CE.reshape(96, 128)
 
@@ -569,7 +592,7 @@
     def middle(level):
         h, b = level.halo, level.block
         level.correct(h - 3, h + b + 3)
-        level.second_step(level.R, level.R, h - 2, h + b + 2)
+        level.second_step(level.R, level.R, h - 2, h + b + 2, h - 2, h + b + 2)
 
         def body(i):
             for j, m in quad(h - 2, h + b + 2):
@@ -595,7 +618,7 @@
     for copy in late0:
         copy.wait_recv()
     L0.correct(1, 21)
-    L0.second_step(L0.R, L0.R, 2, 20)
+    L0.second_step(L0.R, L0.R, 2, 20, 2, 20)
 
     def last(i):
         for j, m in quad(3, 19):
@@ -629,7 +652,7 @@
         copy.wait()
 
 
-def coarse(gx, gy, kinds, CG, CR, CV, KXM, KXP, KA, KB, KZ, CD, CI, CS, CE):
+def coarse(gx, gy, kinds, CG, CR, CV, KXM, KXP, KA, KB, KZ, CD, CI, CSA, CSB, CRB, CE):
     planes = 2 * NX
     scale = 0.25 ** (LEVELS - 1)
     lane = lanes()
@@ -644,8 +667,8 @@
     zeros = jnp.zeros((PAD, 2, 8, 128), F32)
     for place in (0, PAD + planes):
         CV[pl.ds(place, PAD)] = zeros
-        CS[0, pl.ds(place, PAD)] = zeros
-        CS[1, pl.ds(place, PAD)] = zeros
+        CSA[pl.ds(place, PAD)] = zeros
+        CSB[pl.ds(place, PAD)] = zeros
 
     def take(b):
         for q in range(BLOCK):
@@ -694,40 +717,52 @@
             CD[here, y] = total
             inverse = 1.0 / total
             CI[here, y] = inverse
-            CS[0, here, y] = CR[here, y] * inverse * (1.0 / CMID)
+            CSA[here, y] = CR[here, y] * inverse * (1.0 / CMID)
 
     blocks(25, setup)
 
     own = pl.ds(PAD - 2 + 2 * gx, 6)
-    CE[...] = CS[0, own]
-
-    def sweep(k, rho):
-        now, later = lax.rem(k, 2), lax.rem(k + 1, 2)
+    CE[...] = CSA[own]
+
+    def sweep(rho, reach, now, later, r_now, r_later):
         rho_next = 1.0 / (2.0 * CSIG - rho)
         step_a = rho_next * rho
         step_b = rho_next * (2.0 / CRAD)
-
-        def body(b):
-            here = pl.ds(PAD + BLOCK * b, BLOCK)
-            prev, after = pl.ds(PAD - 1 + BLOCK * b, BLOCK), pl.ds(PAD + 1 + BLOCK * b, BLOCK)
-            even, odd = CS[now, here, 0], CS[now, here, 1]
+        size = 6 + 2 * reach
+        start = PAD + jnp.minimum(jnp.maximum(2 * gx - 2 - reach, 0), planes - size)
+        for first in range(0, size, PLANES):
+            count = min(PLANES, size - first)
+            here = pl.ds(start + first, count)
+            prev, after = pl.ds(start + first - 1, count), pl.ds(start + first + 1, count)
+            even, odd = now[here, 0], now[here, 1]
             ka, kb = KA[here], KB[here]
             for y, value, beside in (
                 (0, even, ka * odd + roll_sub(kb * odd, 1)),
                 (1, odd, ka * even + kb * roll_sub(even, -1)),
             ):
                 kz = KZ[here, y]
-                near = KXM[here, y] * CS[now, prev, y] + KXP[here, y] * CS[now, after, y] + beside
+                near = KXM[here, y] * now[prev, y] + KXP[here, y] * now[after, y] + beside
                 near = near + (kz * roll_lane(value, -1) + roll_lane(kz * value, 1))
-                r = CR[here, y] - CD[here, y] * value + near
-                CR[here, y] = r
-                CS[later, here, y] = tiled(step_a, r) * value + tiled(step_b, r) * (r * CI[here, y])
-
-        blocks(CSWEEPS - 2 - k, body)
-        CE[...] = CE[...] + CS[later, own]
+                r = r_now[here, y] - CD[here, y] * value + near
+                r_later[here, y] = r
+                later[here, y] = tiled(step_a, r) * value + tiled(step_b, r) * (r * CI[here, y])
+        CE[...] = CE[...] + later[own]
         return rho_next
 
-    lax.fori_loop(0, CSWEEPS - 1, sweep, jnp.full((8, 128), 1.0 / CSIG, F32))
+    def two(reach):
+        def body(_, rho):
+            rho = sweep(rho, reach, CSA, CSB, CR, CRB)
+            return sweep(rho, reach, CSB, CSA, CRB, CR)
+
+        return body
+
+    rho = jnp.full((8, 128), 1.0 / CSIG, F32)
+    for first in range(0, CSWEEPS - 1, 4):
+        reach = CSWEEPS - 2 - first
+        pairs = min(4, CSWEEPS - 1 - first) // 2
+        rho = lax.fori_loop(0, pairs, two(reach), rho)
+    if (CSWEEPS - 1) % 2:
+        sweep(rho, 0, CSA, CSB, CR, CRB)
 
 
 def per_device(body_force, phase, viscosity_table, wall_kinds):
@@ -741,7 +776,7 @@
         vmem(), pltpu.VMEM((16, 2, 32, 128), F32),
     ]
     depth = 2 * NX + 2 * PAD
-    scratch += [vmem(depth, 2)] * 4 + [vmem(depth)] * 2 + [vmem(depth, 2)] * 3 + [vmem(2, depth, 2), vmem(6, 2)]
+    scratch += [vmem(depth, 2)] * 4 + [vmem(depth)] * 2 + [vmem(depth, 2)] * 3 + [vmem(depth, 2)] * 3 + [vmem(6, 2)]
     scratch += [vmem(16, 16)]
     for frame in (22, 16, 12):
         scratch += [vmem(frame, frame)] * 12

time: 80.4 us -> 73.6 us (0.915); the launches traced: 80.3 us -> 72.4 us
  Pallas kernels: 76.6 us -> 68.7 us
    pallas_call x1, Pallas kernels: 76.6 us -> 68.7 us  [per_device(): pl.pallas_call(kernel, out_shape=(shape, shape), in_specs=[pl.BlockSpec(m...]
where the time goes in v3:
time: 73.6 us; the launch traced here: 72.4 us
  Pallas kernels  68.7 us (93%)
  local copies, waits for them, and re-layouts  3.02 us (4%)
    pallas_call x1, Pallas kernels, per_device(): pl.pallas_call(kernel, out_shape=(shape, shape), in_specs=[pl.BlockSpec(m...  68.7 us
    unnamed x4, local copies, waits for them, and re-layouts  3.02 us

profile of v3, /device:TPU:3, one launch (start us, length us, event | category | flops | bytes accessed | tf_op | source)
XLA Modules:
  0.0 72.4 jit_solution(1114627625403340473)
XLA Ops:
  0.6 68.7 %vcycle.1 = (f32[3,16,16,256]{3,2,1,0:T(8,128)}, f32[3,16,16,256]{3,2,1,0:T(8,128)}) custom-call(f32[3,16,16,256]{3,2,1,0:T(8,128)} %force.1, s32[16,16,256]{2,1,0:T(8,128)} %phase.1, f32[8]{0:T(128)} %table.1, s32[3,6]{1,0:T(4,128)} %kinds.1), custom_call_target="tpu_custom_call" | custom-call | tf_op jit(solution)/shard_map/vcycle/pallas_call | solution.py:786
  69.4 0.0 copy-start
  69.4 2.1 %copy.8 = f32[3,16,16,256]{3,2,1,0:T(8,128)} copy(f32[3,16,16,256]{3,2,1,0:T(8,128)} %get-tuple-element.4) | data formatting | bytes 1572864
  71.5 0.0 copy-done
  71.5 0.9 %copy.9 = f32[3,16,16,256]{3,2,1,0:T(8,128)} copy(f32[3,16,16,256]{3,2,1,0:T(8,128)S(1)} %copy-done) | data formatting | bytes 1572864
Async XLA Ops:
  69.4 2.1 %copy-start = (f32[3,16,16,256]{3,2,1,0:T(8,128)S(1)}, f32[3,16,16,256]{3,2,1,0:T(8,128)}, u32[]{:S(2)}) copy-start(f32[3,16,16,256]{3,2,1,0:T(8,128)} %get-tuple-element.5) | copy-start | bytes 2359300

commit v4 on v3

--- a/solution.py
+++ b/solution.py
@@ -96,7 +96,7 @@
 
 def loop(lo, hi, body, width=CHUNK):
     whole = isinstance(lo, int) and isinstance(hi, int)
-    most = 7 if width <= 4 else 4
+    most = 10
     turns = next(k for k in range(most, 0, -1) if k == 1 or whole and (hi - lo) % k == 0)
 
     def step(t, carry):

time: 73.6 us -> 71.1 us (0.966)
  Pallas kernels: 68.7 us -> 66.2 us
    pallas_call x1, Pallas kernels: 68.7 us -> 66.2 us  [per_device(): pl.pallas_call(kernel, out_shape=(shape, shape), in_specs=[pl.BlockSpec(m...]
where the time goes in v4:
time: 71.1 us; the launch traced here: 69.9 us
  Pallas kernels  66.2 us (93%)
  local copies, waits for them, and re-layouts  3.02 us (4%)
    pallas_call x1, Pallas kernels, per_device(): pl.pallas_call(kernel, out_shape=(shape, shape), in_specs=[pl.BlockSpec(m...  66.2 us
    unnamed x4, local copies, waits for them, and re-layouts  3.02 us

profile of v4, /device:TPU:3, one launch (start us, length us, event | category | flops | bytes accessed | tf_op | source)
XLA Modules:
  0.0 69.9 jit_solution(13132866306276535069)
XLA Ops:
  0.6 66.2 %vcycle.1 = (f32[3,16,16,256]{3,2,1,0:T(8,128)}, f32[3,16,16,256]{3,2,1,0:T(8,128)}) custom-call(f32[3,16,16,256]{3,2,1,0:T(8,128)} %force.1, s32[16,16,256]{2,1,0:T(8,128)} %phase.1, f32[8]{0:T(128)} %table.1, s32[3,6]{1,0:T(4,128)} %kinds.1), custom_call_target="tpu_custom_call" | custom-call | tf_op jit(solution)/shard_map/vcycle/pallas_call | solution.py:786
  66.9 0.0 copy-start
  66.9 2.1 %copy.8 = f32[3,16,16,256]{3,2,1,0:T(8,128)} copy(f32[3,16,16,256]{3,2,1,0:T(8,128)} %get-tuple-element.4) | data formatting | bytes 1572864
  69.0 0.0 copy-done
  69.0 0.9 %copy.9 = f32[3,16,16,256]{3,2,1,0:T(8,128)} copy(f32[3,16,16,256]{3,2,1,0:T(8,128)S(1)} %copy-done) | data formatting | bytes 1572864
Async XLA Ops:
  66.9 2.1 %copy-start = (f32[3,16,16,256]{3,2,1,0:T(8,128)S(1)}, f32[3,16,16,256]{3,2,1,0:T(8,128)}, u32[]{:S(2)}) copy-start(f32[3,16,16,256]{3,2,1,0:T(8,128)} %get-tuple-element.5) | copy-start | bytes 2359300

commit v5 on v4

--- a/solution.py
+++ b/solution.py
@@ -629,23 +629,20 @@
             L0.R[i, here] = L0.R[i, here] - diag * step + near
             OW[i - 3, pl.ds(j - 3, m)] = diag * field
 
-    loop(3, 19, last)
     stores = []
-    for c in range(3):
-        for s in range(2):
-            place = pl.ds(128 * s, 128)
-            stores.append(
-                pltpu.make_async_copy(OW.at[:, :, 2 * c + s], out_w.at[c, :, :, place], in_sem.at[len(stores)])
-            )
-            stores.append(
-                pltpu.make_async_copy(
-                    L0.R.at[pl.ds(3, 16), pl.ds(3, 16), 2 * c + s],
-                    out_r.at[c, :, :, place],
-                    in_sem.at[len(stores)],
-                )
-            )
-    for copy in stores:
-        copy.start()
+    for half in range(2):
+        loop(3 + 8 * half, 11 + 8 * half, last)
+        rows = pl.ds(8 * half, 8)
+        for c in range(3):
+            for s in range(2):
+                spot = pl.ds(128 * s, 128)
+                for src, dst in (
+                    (OW.at[rows, :, 2 * c + s], out_w),
+                    (L0.R.at[pl.ds(3 + 8 * half, 8), pl.ds(3, 16), 2 * c + s], out_r),
+                ):
+                    copy = pltpu.make_async_copy(src, dst.at[c, rows, :, spot], in_sem.at[len(stores)])
+                    copy.start()
+                    stores.append(copy)
     for copy in sent:
         copy.wait_send()
     for copy in stores:
@@ -781,7 +778,7 @@
     for frame in (22, 16, 12):
         scratch += [vmem(frame, frame)] * 12
     n_sems = 107
-    scratch += [pltpu.SemaphoreType.DMA((14,)), pltpu.SemaphoreType.DMA((n_sems,)), pltpu.SemaphoreType.DMA((n_sems,))]
+    scratch += [pltpu.SemaphoreType.DMA((24,)), pltpu.SemaphoreType.DMA((n_sems,)), pltpu.SemaphoreType.DMA((n_sems,))]
     shape = jax.ShapeDtypeStruct(body_force.shape, F32)
     return pl.pallas_call(
         kernel,

time: 71.1 us -> 70.8 us (level)
  no operation moved by 1% of the time
where the time goes in v5:
time: 70.8 us; the launch traced here: 69.7 us
  Pallas kernels  66 us (93%)
  local copies, waits for them, and re-layouts  3.02 us (4%)
    pallas_call x1, Pallas kernels, per_device(): pl.pallas_call(kernel, out_shape=(shape, shape), in_specs=[pl.BlockSpec(m...  66 us
    unnamed x4, local copies, waits for them, and re-layouts  3.02 us

profile of v5, /device:TPU:3, one launch (start us, length us, event | category | flops | bytes accessed | tf_op | source)
XLA Modules:
  0.0 69.7 jit_solution(1076272989480582504)
XLA Ops:
  0.6 66.0 %vcycle.1 = (f32[3,16,16,256]{3,2,1,0:T(8,128)}, f32[3,16,16,256]{3,2,1,0:T(8,128)}) custom-call(f32[3,16,16,256]{3,2,1,0:T(8,128)} %force.1, s32[16,16,256]{2,1,0:T(8,128)} %phase.1, f32[8]{0:T(128)} %table.1, s32[3,6]{1,0:T(4,128)} %kinds.1), custom_call_target="tpu_custom_call" | custom-call | tf_op jit(solution)/shard_map/vcycle/pallas_call | solution.py:783
  66.7 0.0 copy-start
  66.7 2.1 %copy.8 = f32[3,16,16,256]{3,2,1,0:T(8,128)} copy(f32[3,16,16,256]{3,2,1,0:T(8,128)} %get-tuple-element.4) | data formatting | bytes 1572864
  68.8 0.0 copy-done
  68.8 0.9 %copy.9 = f32[3,16,16,256]{3,2,1,0:T(8,128)} copy(f32[3,16,16,256]{3,2,1,0:T(8,128)S(1)} %copy-done) | data formatting | bytes 1572864
Async XLA Ops:
  66.7 2.1 %copy-start = (f32[3,16,16,256]{3,2,1,0:T(8,128)S(1)}, f32[3,16,16,256]{3,2,1,0:T(8,128)}, u32[]{:S(2)}) copy-start(f32[3,16,16,256]{3,2,1,0:T(8,128)} %get-tuple-element.5) | copy-start | bytes 2359300
